TPU v7x, 32 devices: a whole 2x2x4 slice. The times are simulated.
32 devices in a mesh: grp: 2 (over x), row: 8 (over z, y), col: 2 (over core).
Axes of the slice: x: 2, y: 2, z: 4, core: 2. Of those that a mesh axis runs over, the one named last changes fastest.
Arguments:
- start_block: float32 [128, 1024], P(('grp', 'row', 'col')), parts along dimension 0
- tiles: float32 [8192, 4096], P(('grp', 'row', 'col')), parts along dimension 0, as said below
- tile_rows: int32 [8192], P(('grp', 'row', 'col')), parts along dimension 0, may hold values from 0 to 63, as said below
- tile_cols: int32 [8192], P(('grp', 'row', 'col')), parts along dimension 0, may hold values from 0 to 63, as said below
- counts: int32 [32], P(('grp', 'row', 'col')), parts along dimension 0, may hold values from 85 to 256, as said below
Outputs:
- basis: float32 [128, 1024], P(('grp', 'row', 'col')), parts along dimension 0
- coefficients: float32 [8, 16, 16], P('grp'), parts along dimension 0
There are 2 independent parts, one for each index of `grp`. A program takes and returns all parts, laid end to end along the dimension named above; each array names one. Nothing has to cross between parts.
Inputs may be any that keep to these rules, and one draw needn't show every extreme that they name: Device d = r * 2 + c (r its row index, c its col index) holds slots d * 256 to (d + 1) * 256 - 1; each such slot's tile_rows lies in [r * 2 * 4, (r + 1) * 2 * 4). For the slots of device d = r * 2 + c, tile_cols >= tile_rows and (tile_cols // 4) % 2 == c. Only the first counts[d] slots of device d are live; some device has 256 live slots. `tiles`: entries have row scales that differ from block row to block row.
All inputs are finite; a program needn't handle non-finite values.
Results may differ from a plain program's by a relative error of at most 0.00012.
Values sent between devices are 32-bit elements; how exact they have to be, the bound alone decides.
A program may use at most 64 MiB of HBM per device.

v0:
```python
import jax
import jax.numpy as jnp
from jax import lax
from jax.sharding import PartitionSpec as P

BS = 64
K = 16


highest = lax.Precision.HIGHEST


def gram_of(left_block, right_block):
    return jnp.einsum("jkb,jlb->kl", left_block, right_block, precision=highest)


def mix(matrix, stacked):
    return jnp.einsum("lk,jlb->jkb", matrix, stacked, precision=highest)


def factor(gram_matrix):
    lower_factor = jnp.linalg.cholesky(gram_matrix)
    identity = jnp.eye(gram_matrix.shape[0], dtype=gram_matrix.dtype)
    inverse_factor = lax.linalg.triangular_solve(lower_factor, identity, left_side=True, lower=True)
    return (lower_factor, inverse_factor)


def per_device(start_block, tiles, tile_rows, tile_cols, counts):
    piece_blocks = start_block.shape[0]
    col_devices = lax.axis_size("col")
    total_rows = float(piece_blocks * lax.axis_size("row") * col_devices * BS)
    slot_count = tile_rows.shape[0]
    alive_mask = (jnp.arange(slot_count, dtype=jnp.int32) < counts[0]).astype(jnp.float32)[
        :, None, None
    ]
    tile_stack = tiles.reshape(slot_count, BS, BS)

    def products(source_cols, source_rows):
        front = jnp.einsum("cab,ckb->cka", tile_stack, source_cols, precision=highest) * alive_mask
        back = jnp.einsum("cab,cka->ckb", tile_stack, source_rows, precision=highest) * alive_mask
        return (front, back)

    def operate(stacked):
        flat = stacked.reshape(piece_blocks, K * BS)
        gathered = lax.all_gather(flat, ("row", "col"), axis=0, tiled=True).reshape(-1, K, BS)
        block_count = gathered.shape[0]
        front, back = products(gathered[tile_cols], gathered[tile_rows])
        partial_value = jax.ops.segment_sum(front, tile_rows, block_count) + jax.ops.segment_sum(
            back, tile_cols, block_count
        )
        result = lax.psum_scatter(
            partial_value.reshape(block_count, K * BS),
            ("row", "col"),
            scatter_dimension=0,
            tiled=True,
        )
        return result.reshape(piece_blocks, K, BS)

    def advance(current, product_block):
        projection = lax.psum(gram_of(current, product_block), ("row", "col")) / total_rows
        residual = product_block - mix(projection, current)
        gram_matrix = lax.psum(gram_of(residual, residual), ("row", "col")) / total_rows
        lower_factor, inverse_factor = factor(gram_matrix)
        return (mix(inverse_factor.T, residual), projection, lower_factor)

    start = start_block.reshape(piece_blocks, K, BS)
    initial = lax.psum(gram_of(start, start), ("row", "col")) / total_rows
    unused_factor, inverse_start = factor(initial)
    first_basis = mix(inverse_start.T, start)
    second_basis, first_proj, first_lower = advance(first_basis, operate(first_basis))
    third_basis, second_proj, second_lower = advance(
        second_basis, operate(second_basis) - mix(first_lower, first_basis)
    )
    return (
        third_basis.reshape(piece_blocks, K * BS),
        jnp.stack([first_proj, first_lower, second_proj, second_lower]),
    )


def solution(mesh):
    return jax.shard_map(
        per_device,
        mesh=mesh,
        in_specs=(
            P(("grp", "row", "col"), None),
            P(("grp", "row", "col"), None),
            P(("grp", "row", "col")),
            P(("grp", "row", "col")),
            P(("grp", "row", "col")),
        ),
        out_specs=(P(("grp", "row", "col"), None), P("grp", None, None)),
        check_vma=False,
    )
```

profile of v0, /device:TPU:1, one launch (start us, length us, event | category | flops | bytes accessed | tf_op | source)
XLA Modules:
  0.0 545.5 jit_solution(8859295509785037581)
XLA Ops:
  7.2 0.8 reshape.53
  8.2 31.1 %psum.35 = f32[16,16]{1,0:T(8,128)S(1)} all-reduce(f32[16,16]{1,0:T(8,128)S(1)} %convolution_bitcast_fusion.13), channel_id=1, replica_groups=mesh['grp'=2,'row'=8,'col'=2] {'row','col'}, use_global_device_ids=true, to_apply=%region_0.0 | all-reduce | flops 256 | bytes 2048 | tf_op jit(solution)/shard_map/psum | solution.py:67
  39.4 1.5 cholesky.59
  40.9 0.6 compare_reduce_fusion.2
  41.5 0.6 fusion.6
  42.2 1.2 custom-call.7
  43.9 22.1 %all-gather = f32[16,4,1024]{2,1,0:T(4,128)S(1)} all-gather(f32[1,4,1024]{2,1,0:T(4,128)S(1)} %reshape.140), channel_id=1, replica_groups=mesh['grp'=2,'row'=8,'col'=2] {'row','col'}, dimensions={0}, use_global_device_ids=true | all-gather | bytes 278528 | tf_op jit(solution)/shard_map/all_gather | solution.py:45
  66.0 0.2 reshape.55
  66.2 0.7 compare_select_fusion.1
  66.9 5.6 %copy.32 = f32[256,4096]{0,1:T(8,128)} copy(f32[256,4096]{1,0:T(8,128)} %param.9) | data formatting | bytes 8388608 | tf_op args[1]
  72.5 9.2 %copy.33 = f32[256,64,64]{2,1,0:T(8,128)} copy(f32[256,64,64]{0,2,1:T(8,128)} %bitcast.109) | data formatting | bytes 8388608 | tf_op jit(solution)/shard_map/reshape | solution.py:36
  82.4 2.3 gather_fusion
  84.7 1.0 gather_fusion.1
  85.7 16.7 %convolution_multiply_fusion.3 = f32[256,16,64]{2,1,0:T(8,128)} fusion(f32[256,16,64]{2,1,0:T(8,128)} %gather_fusion, f32[256,64,64]{2,1,0:T(8,128)} %copy.33, f32[256]{0:T(256)S(1)} %compare_convert_fusion), kind=kOutput, calls=%fused_computation.11 | convolution fusion | flops 201588736 | bytes 6292480 | tf_op jit(solution)/shard_map/cab,ckb->cka/dot_general | solution.py:39
  102.5 10.5 %convolution_multiply_fusion.2 = f32[256,16,64]{2,1,0:T(8,128)} fusion(f32[256,16,64]{2,1,0:T(8,128)S(1)} %gather_fusion.1, f32[256,64,64]{2,1,0:T(8,128)} %copy.33, f32[256]{0:T(256)S(1)} %compare_convert_fusion), kind=kOutput, calls=%fused_computation.10 | convolution fusion | flops 201588736 | bytes 6292480 | tf_op jit(solution)/shard_map/cab,cka->ckb/dot_general | solution.py:40
  113.0 20.7 %scatter_fusion = f32[64,16,64]{2,1,0:T(8,128)S(1)} fusion(f32[64,16,64]{2,1,0:T(8,128)S(1)} %broadcast.53.clone.1, s32[256]{0:T(256)S(1)} %copy-done.3, f32[256,16,64]{2,1,0:T(8,128)} %convolution_multiply_fusion.3), kind=kCustom, calls=%fused_computation.4 | custom fusion | flops 262144 | bytes 3146752 | tf_op jit(solution)/shard_map/scatter-add | solution.py:48
  133.8 9.2 %scatter_fusion.1 = f32[64,16,64]{2,1,0:T(8,128)S(1)} fusion(f32[64,16,64]{2,1,0:T(8,128)S(1)} %broadcast.53.clone.2, s32[256]{0:T(256)S(1)} %copy-done.2, f32[256,16,64]{2,1,0:T(8,128)S(1)} %copy-done.1), kind=kCustom, calls=%fused_computation.5 | custom fusion | flops 262144 | bytes 3146752 | tf_op jit(solution)/shard_map/scatter-add | solution.py:48
  143.0 0.9 reshape.57
  144.0 0.6 dynamic-slice
  145.2 87.2 %all-reduce.5.cloned.1.call-done = f32[64,1024]{1,0:T(8,128)} async-done(((f32[64,1024]{1,0:T(8,128)}), f32[64,1024]{1,0:T(8,128)}) %all-reduce.5.cloned.1.call-update) | async-done | bytes 262160
  232.4 0.8 constant_dynamic-slice_fusion.1
  233.4 29.3 %psum.36 = f32[16,16]{1,0:T(8,128)S(1)} all-reduce(f32[16,16]{1,0:T(8,128)S(1)} %convolution_bitcast_fusion.11), channel_id=1, replica_groups=mesh['grp'=2,'row'=8,'col'=2] {'row','col'}, use_global_device_ids=true, to_apply=%region_6.9 | all-reduce | flops 256 | bytes 2048 | tf_op jit(solution)/shard_map/psum | solution.py:60
  263.1 32.6 %psum.37 = f32[16,16]{1,0:T(8,128)S(1)} all-reduce(f32[16,16]{1,0:T(8,128)S(1)} %convolution_bitcast_fusion.10), channel_id=1, replica_groups=mesh['grp'=2,'row'=8,'col'=2] {'row','col'}, use_global_device_ids=true, to_apply=%region_7.10 | all-reduce | flops 256 | bytes 2048 | tf_op jit(solution)/shard_map/psum | solution.py:62
  295.8 1.5 cholesky.70
  297.3 0.6 compare_reduce_fusion.1
  298.0 0.6 fusion.19
  298.6 1.2 custom-call.8
  300.3 18.3 %all-gather.1 = f32[16,4,1024]{2,1,0:T(4,128)S(1)} all-gather(f32[1,4,1024]{2,1,0:T(4,128)S(1)} %reshape.142), channel_id=1, replica_groups=mesh['grp'=2,'row'=8,'col'=2] {'row','col'}, dimensions={0}, use_global_device_ids=true | all-gather | bytes 278528 | tf_op jit(solution)/shard_map/all_gather | solution.py:45
  318.6 0.2 reshape.60
  318.9 2.3 gather_fusion.3
  321.2 1.0 gather_fusion.2
  322.2 10.9 %convolution_multiply_fusion = f32[256,16,64]{2,1,0:T(8,128)} fusion(f32[256,16,64]{2,1,0:T(8,128)} %gather_fusion.3, f32[256,64,64]{2,1,0:T(8,128)} %copy.33, f32[256]{0:T(256)S(1)} %compare_convert_fusion), kind=kOutput, calls=%fused_computation.8 | convolution fusion | flops 201588736 | bytes 6292480 | tf_op jit(solution)/shard_map/cab,cka->ckb/dot_general | solution.py:40
  333.1 16.4 %convolution_multiply_fusion.1 = f32[256,16,64]{2,1,0:T(8,128)} fusion(f32[256,16,64]{2,1,0:T(8,128)S(1)} %gather_fusion.2, f32[256,64,64]{2,1,0:T(8,128)} %copy.33, f32[256]{0:T(256)S(1)} %compare_convert_fusion), kind=kOutput, calls=%fused_computation.9 | convolution fusion | flops 201588736 | bytes 6292480 | tf_op jit(solution)/shard_map/cab,ckb->cka/dot_general | solution.py:39
  349.5 20.4 %scatter_fusion.3 = f32[64,16,64]{2,1,0:T(8,128)S(1)} fusion(f32[64,16,64]{2,1,0:T(8,128)S(1)} %broadcast.53.clone.3, s32[256]{0:T(256)S(1)} %copy-done.2, f32[256,16,64]{2,1,0:T(8,128)} %convolution_multiply_fusion), kind=kCustom, calls=%fused_computation.7 | custom fusion | flops 262144 | bytes 3146752 | tf_op jit(solution)/shard_map/scatter-add | solution.py:48
  370.0 9.2 %scatter_fusion.2 = f32[64,16,64]{2,1,0:T(8,128)S(1)} fusion(f32[64,16,64]{2,1,0:T(8,128)S(1)} %broadcast.53.clone, s32[256]{0:T(256)S(1)} %copy-done.3, f32[256,16,64]{2,1,0:T(8,128)S(1)} %copy-done), kind=kCustom, calls=%fused_computation.6 | custom fusion | flops 262144 | bytes 3146752 | tf_op jit(solution)/shard_map/scatter-add | solution.py:48
  379.3 0.9 reshape.61
  380.2 88.4 %all-reduce.7.cloned.1.call-done = f32[64,1024]{1,0:T(8,128)} async-done(((f32[64,1024]{1,0:T(8,128)}), f32[64,1024]{1,0:T(8,128)}) %all-reduce.7.cloned.1.call-update) | async-done | bytes 262160
  468.6 0.8 constant_dynamic-slice_fusion
  469.5 0.9 fusion.1
  470.5 29.3 %psum.38 = f32[16,16]{1,0:T(8,128)S(1)} all-reduce(f32[16,16]{1,0:T(8,128)S(1)} %convolution_bitcast_fusion.8), channel_id=1, replica_groups=mesh['grp'=2,'row'=8,'col'=2] {'row','col'}, use_global_device_ids=true, to_apply=%region_11.14 | all-reduce | flops 256 | bytes 2048 | tf_op jit(solution)/shard_map/psum | solution.py:60
  499.8 0.2 fusion
  500.2 32.6 %psum.39 = f32[16,16]{1,0:T(8,128)S(1)} all-reduce(f32[16,16]{1,0:T(8,128)S(1)} %convolution_bitcast_fusion.7), channel_id=1, replica_groups=mesh['grp'=2,'row'=8,'col'=2] {'row','col'}, use_global_device_ids=true, to_apply=%region_12.15 | all-reduce | flops 256 | bytes 2048 | tf_op jit(solution)/shard_map/psum | solution.py:62
  533.0 1.5 cholesky.81
  534.4 0.6 compare_reduce_fusion
  535.1 0.6 fusion.18
  535.8 1.2 custom-call.9
  537.4 0.7 reshape.63
  538.1 0.6 pad_maximum_fusion
  (57 shorter events, 3.4 us)
Async XLA Ops:
  7.2 225.2 %all-reduce.5.cloned.1.call-start = ((), (), s32[]{:S(2)}) async-start(), calls=%async_computation | async-start | bytes 524288
  72.5 9.8 %copy-start.3 = (s32[256]{0:T(256)S(1)}, s32[256]{0:T(256)}, u32[]{:S(2)}) copy-start(s32[256]{0:T(256)} %param.10) | copy-start | bytes 3076
  113.0 20.7 %copy-start.1 = (f32[256,16,64]{2,1,0:T(8,128)S(1)}, f32[256,16,64]{2,1,0:T(8,128)}, u32[]{:S(2)}) copy-start(f32[256,16,64]{2,1,0:T(8,128)} %convolution_multiply_fusion.2) | copy-start | bytes 3145732
  113.0 20.7 %copy-start.2 = (s32[256]{0:T(256)S(1)}, s32[256]{0:T(256)}, u32[]{:S(2)}) copy-start(s32[256]{0:T(256)} %param.11) | copy-start | bytes 3076
  142.9 1.1 copy-start.4
  143.9 324.7 %all-reduce.7.cloned.1.call-start = ((), (), s32[]{:S(2)}) async-start(), calls=%async_computation.1 | async-start | bytes 524288
  349.5 20.5 %copy-start = (f32[256,16,64]{2,1,0:T(8,128)S(1)}, f32[256,16,64]{2,1,0:T(8,128)}, u32[]{:S(2)}) copy-start(f32[256,16,64]{2,1,0:T(8,128)} %convolution_multiply_fusion.1) | copy-start | bytes 3145732
Sparse Core Ops, SparseCore 0:
  144.1 88.2 all-reduce.4
  380.3 88.2 all-reduce.6
where the time goes:
time: 547 us; the launch traced here: 546 us
  blocking collectives  195 us (36%)
  waiting for transfers between devices  176 us (32%)
  other arithmetic  73 us (13%)
  matrix products  57.7 us (11%)
  local copies, waits for them, and re-layouts  28.2 us (5%)
  between operations  15.7 us (3%)
    unnamed x4, waiting for transfers between devices  176 us
    psum x2, blocking collectives, advance(): lax.psum(gram_of(residual, residual), ('row', 'col')) / total_rows  65.2 us
    psum x2, blocking collectives, advance(): lax.psum(gram_of(current, product_block), ('row', 'col')) / total_rows  58.6 us
    all_gather x2, blocking collectives, operate(): lax.all_gather(flat, ('row', 'col'), axis=0, tiled=True).reshape(-1, K, BS)  40.4 us
    dot_general x2, matrix products, products(): jnp.einsum('cab,ckb->cka', tile_stack, source_cols, precision=highest)  33.1 us
    psum x1, blocking collectives, per_device(): initial = lax.psum(gram_of(start, start), ('row', 'col')) / total_rows  31.1 us
    scatter-add x2, other arithmetic, operate(): jax.ops.segment_sum(front, tile_rows, block_count)  29.9 us
    scatter-add x2, other arithmetic, operate(): jax.ops.segment_sum(back, tile_cols, block_count)  29.6 us
  transfers between devices with their start and end apart: 2, of which 2 were waited for; matrix products, arithmetic and copies ran while one was open for 0% of the time, Pallas kernels for 0%

commit v1 on v0

v1 whole, which is shorter than its diff:
```python
import functools

import jax
import jax.numpy as jnp
from jax import lax
from jax.experimental import pallas as pl
from jax.experimental.pallas import tpu as pltpu
from jax.sharding import PartitionSpec as P

BS = 64
K = 16
F32 = jnp.float32
BF16 = jnp.bfloat16
MESH = pl.DeviceIdType.MESH
HIGHEST = lax.Precision.HIGHEST


def dot_nn(a, b):
    precision = HIGHEST if a.dtype == F32 else None
    return lax.dot_general(a, b, (((1,), (0,)), ((), ())), precision=precision, preferred_element_type=F32)


def dot_nt(a, b):
    precision = HIGHEST if a.dtype == F32 else None
    return lax.dot_general(a, b, (((1,), (1,)), ((), ())), precision=precision, preferred_element_type=F32)


def split2(x):
    high = x.astype(BF16)
    return high, (x - high.astype(F32)).astype(BF16)


def split3(x):
    high = x.astype(BF16)
    rest = x - high.astype(F32)
    middle = rest.astype(BF16)
    return high, middle, (rest - middle.astype(F32)).astype(BF16)


def factor(gram):
    row = lax.broadcasted_iota(jnp.int32, (K, K), 0)
    col = lax.broadcasted_iota(jnp.int32, (K, K), 1)
    upper = gram
    inverse = (row == col).astype(F32)
    for j in range(K):
        ratio = upper[:, j : j + 1] / upper[j : j + 1, j : j + 1]
        ratio = jnp.where(row > j, jnp.broadcast_to(ratio, (K, K)), 0.0)
        upper, inverse = upper - ratio * upper[j : j + 1, :], inverse - ratio * inverse[j : j + 1, :]
    diagonal = jnp.sum(jnp.where(row == col, upper, 0.0), axis=1, keepdims=True)
    scale = 1.0 / jnp.sqrt(diagonal)
    return jnp.where(col >= row, upper * scale, 0.0), inverse * scale


def kernel(
    rows_n, cols_n, pb,
    start, tiles, tile_rows, tile_cols, counts, basis, coef,
    f0, f1, f2, fq1, fw, fq2, dh, dl, lext, permt, chunk, piece, fb, sb, rs, rsib, acc,
    ags, agf, agr, rss, rsr, sibs, sibr,
):
    r = lax.axis_index("row")
    c = lax.axis_index("col")
    other = 1 - c
    piece_lanes = pb * BS
    total = float(rows_n * cols_n * piece_lanes)
    row_blocks = cols_n * pb
    row_lanes = row_blocks * BS
    pairs = BS // 2

    barrier = pltpu.get_barrier_semaphore()
    pl.semaphore_signal(barrier, inc=1, device_id={"row": r, "col": other}, device_id_type=MESH)
    for i in range(1, rows_n):
        pl.semaphore_signal(
            barrier, inc=1, device_id={"row": lax.rem(r + i, rows_n), "col": c}, device_id_type=MESH
        )

    lane = lax.broadcasted_iota(jnp.int32, (8, 128), 1)

    def lanes_of(col, row):
        return pl.ds(pl.multiple_of((col * rows_n + row) * piece_lanes, 128), piece_lanes)

    own = lanes_of(c, r)

    for j in range(pb):
        for m in range(K // 2):
            chunk[j * 8 + m : j * 8 + m + 1, :] = start[j : j + 1, m * 128 : (m + 1) * 128]
    for jp in range(pb // 2):
        one = chunk[jp * 16 : jp * 16 + 8, :]
        two = chunk[jp * 16 + 8 : jp * 16 + 16, :]
        piece[jp, pl.ds(0, 8, stride=2), :] = jnp.where(
            lane < 64, one, pltpu.roll(two, 64, 1)
        )
        piece[jp, pl.ds(1, 8, stride=2), :] = jnp.where(
            lane < 64, pltpu.roll(one, 64, 1), two
        )
    f0[:, own] = jnp.concatenate([piece[jp] for jp in range(pb // 2)], axis=1)

    def ag_copy(ref, ph, col, row, send_sem, target_row, target_col):
        return pltpu.make_async_remote_copy(
            src_ref=ref.at[:, lanes_of(col, row)],
            dst_ref=ref.at[:, lanes_of(col, row)],
            send_sem=send_sem,
            recv_sem=agr.at[ph, col, row],
            device_id={"row": target_row, "col": target_col},
            device_id_type=MESH,
        )

    def ag_start(ref, ph):
        for i in range(rows_n - 1, 0, -1):
            ag_copy(ref, ph, c, r, ags.at[ph, i], lax.rem(r + i, rows_n), c).start()
        ag_copy(ref, ph, c, r, ags.at[ph, 0], r, other).start()

    def ag_forward(ref, ph):
        for i in range(1, rows_n):
            source = lax.rem(r + i, rows_n)
            copy = ag_copy(ref, ph, c, source, agf.at[ph, i], r, other)
            copy.wait_recv()
            copy.start()

    def ag_end(ref, ph):
        for i in range(rows_n):
            source = lax.rem(r + i, rows_n)
            ag_copy(ref, ph, other, source, agf.at[ph, i], r, other).wait_recv()

    def ag_drain(ref, ph):
        for i in range(1, rows_n):
            ag_copy(ref, ph, c, r, ags.at[ph, i], lax.rem(r + i, rows_n), c).wait_send()
            ag_copy(ref, ph, c, lax.rem(r + i, rows_n), agf.at[ph, i], r, other).wait_send()
        ag_copy(ref, ph, c, r, ags.at[ph, 0], r, other).wait_send()

    def rs_copy(ph, source, target):
        return pltpu.make_async_remote_copy(
            src_ref=sb.at[ph, target],
            dst_ref=rs.at[ph, source],
            send_sem=rss.at[ph, target],
            recv_sem=rsr.at[ph, source],
            device_id={"row": target, "col": c},
            device_id_type=MESH,
        )

    def half(col):
        return pl.ds(pl.multiple_of(col * piece_lanes, 128), piece_lanes)

    def sib_copy(ph):
        return pltpu.make_async_remote_copy(
            src_ref=fb.at[ph, :, half(other)],
            dst_ref=rsib.at[ph],
            send_sem=sibs.at[ph],
            recv_sem=sibr.at[ph],
            device_id={"row": r, "col": other},
            device_id_type=MESH,
        )

    pl.semaphore_wait(barrier, rows_n)
    ag_start(f0, 0)

    q = lax.broadcasted_iota(jnp.int32, (row_blocks * pairs, row_lanes), 0)
    p = lax.broadcasted_iota(jnp.int32, (row_blocks * pairs, row_lanes), 1)
    place = (q % row_blocks) * BS + (q // row_blocks) * 2
    permt[0] = (p == place).astype(F32).astype(BF16)
    permt[1] = (p == place + 1).astype(F32).astype(BF16)

    slots = tile_rows.shape[1]
    places = rows_n * pb * row_blocks
    tr = tile_rows[...]
    tc = tile_cols[...]
    position = (
        ((tc // (pb * cols_n)) * pb + tc % pb) * row_blocks + (tr - r * row_blocks)
    )
    slot = lax.broadcasted_iota(jnp.int32, (1, slots), 1)
    position = jnp.where(slot < counts[0], position, -1)
    pick = (lax.broadcasted_iota(jnp.int32, (places, slots), 0) == position).astype(F32).astype(BF16)

    def densify(i, carry):
        high, low = split2(tiles[:, pl.ds(pl.multiple_of(i * 256, 256), 256)])
        x = dot_nn(pick, high) + dot_nn(pick, low)
        for j in range(rows_n * pb):
            block = x[j * 8 : (j + 1) * 8]
            high, low = split2(jnp.concatenate([block[:, :128], block[:, 128:]], axis=0))
            at = pl.ds(pl.multiple_of(i * 16, 16), 16)
            dh[at, j * 128 : (j + 1) * 128] = high
            dl[at, j * 128 : (j + 1) * 128] = low
        return carry

    lax.fori_loop(0, pairs // 2, densify, 0)

    def product(ref, ph):
        across = jnp.concatenate([ref[:, lanes_of(i, r)] for i in range(cols_n)], axis=1)
        parts = jnp.concatenate(split3(across), axis=0)
        even = dot_nt(parts, permt[0]).astype(BF16)
        odd = dot_nt(parts, permt[1]).astype(BF16)
        lrow = jnp.concatenate(
            [x[i * K : (i + 1) * K] for i in range(3) for x in (even, odd)], axis=0
        )
        wide = lax.broadcasted_iota(jnp.int32, (K, 128), 1)
        low_half = wide < 64

        def back(step, carry):
            target = rows_n - 1 - step
            at = pl.ds(pl.multiple_of(target * pb * 128, 128), pb * 128)
            v = ref[:, lanes_of(c, target)]
            extended = []
            for jp in range(pb // 2):
                x = v[:, jp * 128 : (jp + 1) * 128]
                y = pltpu.roll(x, 64, 1)
                extended.append(
                    jnp.concatenate([jnp.where(low_half, x, 0.0), jnp.where(low_half, 0.0, y)], axis=0)
                )
                extended.append(
                    jnp.concatenate([jnp.where(low_half, y, 0.0), jnp.where(low_half, 0.0, x)], axis=0)
                )
            lext[:, at] = jnp.concatenate(split3(jnp.concatenate(extended, axis=1)), axis=0)

            @pl.when(target >= r)
            def _():
                x = dot_nn(lrow, dh[:, at])
                y = dot_nn(lrow[: 4 * K], dl[:, at])
                z = x[4 * K :] + (x[2 * K : 4 * K] + y[2 * K :]) + y[: 2 * K] + x[: 2 * K]
                sums = []
                for j in range(pb):
                    s = jnp.where(
                        low_half, z[:K, j * 128 : (j + 1) * 128], z[K:, j * 128 : (j + 1) * 128]
                    )
                    sums.append(s + pltpu.roll(s, 64, 1))
                sb[ph, target] = jnp.concatenate(
                    [jnp.where(low_half, sums[2 * j], sums[2 * j + 1]) for j in range(pb // 2)], axis=1
                )

            @pl.when(target > r)
            def _():
                rs_copy(ph, r, target).start()

            return carry

        lax.fori_loop(0, rows_n, back, 0)

        x = dot_nt(lext[...], dh[...])
        y = dot_nt(lext[: 4 * K, :], dl[...])
        z = x[4 * K :] + (x[2 * K : 4 * K] + y[2 * K :]) + y[: 2 * K] + x[: 2 * K]
        parts = split3(z)
        out = dot_nn(jnp.concatenate([x[:K] for x in parts], axis=0), permt[0]) + dot_nn(
            jnp.concatenate([x[K:] for x in parts], axis=0), permt[1]
        )
        fb[ph] = out[2 * K :] + out[K : 2 * K] + out[:K]
        sib_copy(ph).start()

    def collect(ph):
        acc[...] = sb[ph, r] + fb[ph, :, half(c)]

        def add(source, carry):
            @pl.when(source < r)
            def _():
                rs_copy(ph, source, r).wait_recv()
                acc[...] += rs[ph, source]

            return carry

        lax.fori_loop(0, rows_n, add, 0)
        sib_copy(ph).wait_recv()
        return acc[...] + rsib[ph]

    def rs_drain(ph):
        def step(target, carry):
            @pl.when(target > r)
            def _():
                rs_copy(ph, r, target).wait_send()

            return carry

        lax.fori_loop(0, rows_n, step, 0)
        sib_copy(ph).wait_send()

    identity = (
        lax.broadcasted_iota(jnp.int32, (K, K), 0) == lax.broadcasted_iota(jnp.int32, (K, K), 1)
    ).astype(F32)

    ag_forward(f0, 0)
    ag_end(f0, 0)
    product(f0, 0)
    v = f0[...]
    unused, inverse0 = factor(dot_nt(v, v) / total)
    fq1[...] = dot_nn(inverse0, v)

    f1[:, own] = collect(0)
    ag_start(f1, 1)
    ag_forward(f1, 1)
    ag_end(f1, 1)
    z1 = dot_nn(inverse0, f1[...])
    q1 = fq1[...]
    a1 = dot_nt(q1, z1) / total
    coef[0] = a1
    fw[...] = z1 - dot_nn(a1.T, q1)
    product(fw, 1)
    w1 = fw[...]
    upper1, inverse1 = factor(dot_nt(w1, w1) / total)
    coef[1] = dot_nt(identity, upper1)
    fq2[...] = dot_nn(inverse1, w1)
    behind = dot_nn(upper1, fq1[:, own])

    f2[:, own] = dot_nn(inverse1, collect(1)) - behind
    ag_start(f2, 2)
    ag_forward(f2, 2)
    ag_end(f2, 2)
    z2 = f2[...]
    q2 = fq2[...]
    a2 = dot_nt(q2, z2) / total
    coef[2] = a2
    a2t = a2.T
    w2 = z2 - dot_nn(a2t, q2)
    upper2, inverse2 = factor(dot_nt(w2, w2) / total)
    coef[3] = dot_nt(identity, upper2)
    piece_out = dot_nn(inverse2, f2[:, own] - dot_nn(a2t, fq2[:, own]))
    for jp in range(pb // 2):
        piece[jp] = piece_out[:, jp * 128 : (jp + 1) * 128]
    for jp in range(pb // 2):
        one = piece[jp, pl.ds(0, 8, stride=2), :]
        two = piece[jp, pl.ds(1, 8, stride=2), :]
        chunk[jp * 16 : jp * 16 + 8, :] = jnp.where(lane < 64, one, pltpu.roll(two, 64, 1))
        chunk[jp * 16 + 8 : jp * 16 + 16, :] = jnp.where(lane < 64, pltpu.roll(one, 64, 1), two)
    for j in range(pb):
        for m in range(K // 2):
            basis[j : j + 1, m * 128 : (m + 1) * 128] = chunk[j * 8 + m : j * 8 + m + 1, :]

    for ph, ref in enumerate((f0, f1, f2)):
        ag_drain(ref, ph)
    for ph in range(2):
        rs_drain(ph)


def solution(mesh):
    rows_n = mesh.shape["row"]
    cols_n = mesh.shape["col"]

    def per_device(start_block, tiles, tile_rows, tile_cols, counts):
        pb = start_block.shape[0]
        slots = tile_rows.shape[0]
        length = rows_n * cols_n * pb * BS
        wide = rows_n * pb * 128
        tall = cols_n * pb * BS // 2
        vmem = pl.BlockSpec(memory_space=pltpu.VMEM)
        return pl.pallas_call(
            functools.partial(kernel, rows_n, cols_n, pb),
            out_shape=(
                jax.ShapeDtypeStruct(start_block.shape, F32),
                jax.ShapeDtypeStruct((4, K, K), F32),
            ),
            in_specs=[vmem] * 4 + [pl.BlockSpec(memory_space=pltpu.SMEM)],
            out_specs=(vmem, vmem),
            scratch_shapes=[pltpu.VMEM((K, length), F32)] * 6
            + [
                pltpu.VMEM((tall, wide), BF16),
                pltpu.VMEM((tall, wide), BF16),
                pltpu.VMEM((6 * K, wide), BF16),
                pltpu.VMEM((2, tall, 2 * tall), BF16),
                pltpu.VMEM((pb * K // 2, 128), F32),
                pltpu.VMEM((pb // 2, K, 128), F32),
                pltpu.VMEM((2, K, cols_n * pb * BS), F32),
                pltpu.VMEM((2, rows_n, K, pb * BS), F32),
                pltpu.VMEM((2, rows_n, K, pb * BS), F32),
                pltpu.VMEM((2, K, pb * BS), F32),
                pltpu.VMEM((K, pb * BS), F32),
                pltpu.SemaphoreType.DMA((3, rows_n)),
                pltpu.SemaphoreType.DMA((3, rows_n)),
                pltpu.SemaphoreType.DMA((3, cols_n, rows_n)),
                pltpu.SemaphoreType.DMA((2, rows_n)),
                pltpu.SemaphoreType.DMA((2, rows_n)),
                pltpu.SemaphoreType.DMA((2,)),
                pltpu.SemaphoreType.DMA((2,)),
            ],
            compiler_params=pltpu.CompilerParams(
                collective_id=0, has_side_effects=True, vmem_limit_bytes=56 * 2**20
            ),
        )(
            start_block,
            tiles,
            tile_rows.reshape(1, slots),
            tile_cols.reshape(1, slots),
            counts,
        )

    return jax.shard_map(
        per_device,
        mesh=mesh,
        in_specs=(
            P(("grp", "row", "col"), None),
            P(("grp", "row", "col"), None),
            P(("grp", "row", "col")),
            P(("grp", "row", "col")),
            P(("grp", "row", "col")),
        ),
        out_specs=(P(("grp", "row", "col"), None), P("grp", None, None)),
        check_vma=False,
    )
```

time: 547 us -> 53.8 us (0.10)
  blocking collectives: 195 us -> 0 us
  waiting for transfers between devices: 176 us -> 0 us
  other arithmetic: 73 us -> 0 us
  matrix products: 57.7 us -> 0 us
  Pallas kernels: 0 us -> 49.6 us
  local copies, waits for them, and re-layouts: 28.2 us -> 2.7 us
  between operations: 15.7 us -> 1.29 us
    unnamed x4 -> x0, waiting for transfers between devices: 176 us -> none
    psum x5 -> x0, blocking collectives: 155 us -> none  [the longest x2 65.2 us: advance(): lax.psum(gram_of(residual, residual), ('row', 'col')) / total_rows]
    scatter-add x4 -> x0, other arithmetic: 59.5 us -> none  [the longest x2 29.9 us: operate(): jax.ops.segment_sum(front, tile_rows, block_count)]
    dot_general x15 -> x0, matrix products: 57.1 us -> none  [the longest x2 33.1 us: products(): jnp.einsum('cab,ckb->cka', tile_stack, source_cols, precision=highest)]
    pallas_call x0 -> x1, Pallas kernels: none -> 49.6 us  [per_device(): pl.pallas_call(functools.partial(kernel, rows_n, cols_n, pb), out_shape=(...]
    all_gather x2 -> x0, blocking collectives: 40.4 us -> none  [operate(): lax.all_gather(flat, ('row', 'col'), axis=0, tiled=True).reshape(-1, K, BS)]
    reshape x9 -> x0, local copies, waits for them, and re-layouts: 13.1 us -> none  [the longest x1 9.16 us: per_device(): tile_stack = tiles.reshape(slot_count, BS, BS)]
    another operation x18 -> x0, other arithmetic: 12.6 us -> none  [the longest x9 6.39 us: factor(): lower_factor = jnp.linalg.cholesky(gram_matrix)]
  transfers between devices with their start and end apart: 2 -> 0, of which waited for: 2 -> 0; matrix products, arithmetic and copies ran while one was open for 0% -> 0% of each run, Pallas kernels for 0% -> 0%
where the time goes in v1:
time: 53.8 us; the launch traced here: 53.6 us
  Pallas kernels  49.6 us (92%)
  local copies, waits for them, and re-layouts  2.7 us (5%)
  between operations  1.29 us (2%)
    pallas_call x1, Pallas kernels, per_device(): pl.pallas_call(functools.partial(kernel, rows_n, cols_n, pb), out_shape=(...  49.6 us
    unnamed x2, local copies, waits for them, and re-layouts  2.7 us

profile of v1, /device:TPU:1, one launch (start us, length us, event | category | flops | bytes accessed | tf_op | source)
XLA Modules:
  0.0 53.6 jit_solution(14675110173828771635)
XLA Ops:
  1.3 49.6 %shard_map.68 = (f32[4,1024]{1,0:T(4,128)}, f32[4,16,16]{2,1,0:T(8,128)}) custom-call(f32[4,1024]{1,0:T(4,128)} %start.1, f32[256,4096]{1,0:T(8,128)} %tiles.1, s32[1,256]{1,0:T(1,128)} %bitcast.2, s32[1,256]{1,0:T(1,128)} %bitcast.3, s32[1]{0:T(128)S(6)} %copy.9.counts), custom_call_target="tpu_custom_call" | custom-call | tf_op jit(solution)/shard_map/pallas_call | solution.py:340
  50.9 1.3 %copy.10 = f32[4,1024]{1,0:T(4,128)} copy(f32[4,1024]{1,0:T(4,128)} %get-tuple-element.4) | data formatting | bytes 32768
  52.2 1.4 %copy.11 = f32[4,16,16]{2,1,0:T(8,128)} copy(f32[4,16,16]{2,1,0:T(8,128)} %get-tuple-element.5) | data formatting | bytes 8192

commit v2 on v1

--- a/solution.py
+++ b/solution.py
@@ -35,6 +35,21 @@
     rest = x - high.astype(F32)
     middle = rest.astype(BF16)
     return high, middle, (rest - middle.astype(F32)).astype(BF16)
+
+
+def parts_of(x):
+    return jnp.concatenate(split3(x), axis=0)
+
+
+def gram_of(left, right):
+    m = dot_nt(left, right)
+    m = m[2 * K :] + m[K : 2 * K] + m[:K]
+    return m[:, 2 * K :] + m[:, K : 2 * K] + m[:, :K]
+
+
+def mix(matrix, parts):
+    out = dot_nn(parts_of(jnp.concatenate([matrix] * 3, axis=1)), parts)
+    return out[2 * K :] + out[K : 2 * K] + out[:K]
 
 
 def factor(gram):
@@ -116,8 +131,8 @@
             copy.wait_recv()
             copy.start()
 
-    def ag_end(ref, ph):
-        for i in range(rows_n):
+    def ag_end(ref, ph, first, last):
+        for i in range(first, last):
             source = lax.rem(r + i, rows_n)
             ag_copy(ref, ph, other, source, agf.at[ph, i], r, other).wait_recv()
 
@@ -194,47 +209,50 @@
         wide = lax.broadcasted_iota(jnp.int32, (K, 128), 1)
         low_half = wide < 64
 
+        group = 4 if rows_n % 4 == 0 else 1
+
         def back(step, carry):
-            target = rows_n - 1 - step
-            at = pl.ds(pl.multiple_of(target * pb * 128, 128), pb * 128)
-            v = ref[:, lanes_of(c, target)]
-            extended = []
-            for jp in range(pb // 2):
-                x = v[:, jp * 128 : (jp + 1) * 128]
-                y = pltpu.roll(x, 64, 1)
-                extended.append(
-                    jnp.concatenate([jnp.where(low_half, x, 0.0), jnp.where(low_half, 0.0, y)], axis=0)
-                )
-                extended.append(
-                    jnp.concatenate([jnp.where(low_half, y, 0.0), jnp.where(low_half, 0.0, x)], axis=0)
-                )
-            lext[:, at] = jnp.concatenate(split3(jnp.concatenate(extended, axis=1)), axis=0)
-
-            @pl.when(target >= r)
-            def _():
+            first = rows_n - (step + 1) * group
+            for g in range(group - 1, -1, -1):
+                target = first + g
+                at = pl.ds(pl.multiple_of(target * pb * 128, 128), pb * 128)
+                v = ref[:, lanes_of(c, target)]
+                extended = []
+                for jp in range(pb // 2):
+                    x = v[:, jp * 128 : (jp + 1) * 128]
+                    y = pltpu.roll(x, 64, 1)
+                    extended.append(
+                        jnp.concatenate([jnp.where(low_half, x, 0.0), jnp.where(low_half, 0.0, y)], axis=0)
+                    )
+                    extended.append(
+                        jnp.concatenate([jnp.where(low_half, y, 0.0), jnp.where(low_half, 0.0, x)], axis=0)
+                    )
+                lext[:, at] = jnp.concatenate(split3(jnp.concatenate(extended, axis=1)), axis=0)
                 x = dot_nn(lrow, dh[:, at])
                 y = dot_nn(lrow[: 4 * K], dl[:, at])
                 z = x[4 * K :] + (x[2 * K : 4 * K] + y[2 * K :]) + y[: 2 * K] + x[: 2 * K]
                 sums = []
                 for j in range(pb):
-                    s = jnp.where(
+                    t = jnp.where(
                         low_half, z[:K, j * 128 : (j + 1) * 128], z[K:, j * 128 : (j + 1) * 128]
                     )
-                    sums.append(s + pltpu.roll(s, 64, 1))
+                    sums.append(t + pltpu.roll(t, 64, 1))
                 sb[ph, target] = jnp.concatenate(
                     [jnp.where(low_half, sums[2 * j], sums[2 * j + 1]) for j in range(pb // 2)], axis=1
                 )
-
-            @pl.when(target > r)
-            def _():
-                rs_copy(ph, r, target).start()
+            for g in range(group - 1, -1, -1):
+                target = first + g
+
+                @pl.when(target > r)
+                def _():
+                    rs_copy(ph, r, target).start()
 
             return carry
 
-        lax.fori_loop(0, rows_n, back, 0)
-
-        x = dot_nt(lext[...], dh[...])
-        y = dot_nt(lext[: 4 * K, :], dl[...])
+        lax.fori_loop(0, rows_n // group, back, 0)
+
+        x = dot_nt(dh[...], lext[...]).T
+        y = dot_nt(dl[...], lext[: 4 * K, :]).T
         z = x[4 * K :] + (x[2 * K : 4 * K] + y[2 * K :]) + y[: 2 * K] + x[: 2 * K]
         parts = split3(z)
         out = dot_nn(jnp.concatenate([x[:K] for x in parts], axis=0), permt[0]) + dot_nn(
@@ -274,41 +292,48 @@
     ).astype(F32)
 
     ag_forward(f0, 0)
-    ag_end(f0, 0)
+    ag_end(f0, 0, 0, 1)
     product(f0, 0)
-    v = f0[...]
-    unused, inverse0 = factor(dot_nt(v, v) / total)
-    fq1[...] = dot_nn(inverse0, v)
+    ag_end(f0, 0, 1, rows_n)
+    v = parts_of(f0[...])
+    unused, inverse0 = factor(gram_of(v, v) / total)
+    fq1[...] = mix(inverse0, v)
 
     f1[:, own] = collect(0)
     ag_start(f1, 1)
     ag_forward(f1, 1)
-    ag_end(f1, 1)
-    z1 = dot_nn(inverse0, f1[...])
-    q1 = fq1[...]
-    a1 = dot_nt(q1, z1) / total
+    ag_end(f1, 1, 0, 1)
+    product(f1, 1)
+    ag_end(f1, 1, 1, rows_n)
+    z1 = mix(inverse0, parts_of(f1[...]))
+    fw[...] = z1
+    q1 = parts_of(fq1[...])
+    a1 = gram_of(q1, parts_of(z1)) / total
     coef[0] = a1
-    fw[...] = z1 - dot_nn(a1.T, q1)
-    product(fw, 1)
-    w1 = fw[...]
-    upper1, inverse1 = factor(dot_nt(w1, w1) / total)
+    a1t = a1.T
+    w1 = parts_of(z1 - mix(a1t, q1))
+    upper1, inverse1 = factor(gram_of(w1, w1) / total)
     coef[1] = dot_nt(identity, upper1)
-    fq2[...] = dot_nn(inverse1, w1)
-    behind = dot_nn(upper1, fq1[:, own])
-
-    f2[:, own] = dot_nn(inverse1, collect(1)) - behind
+    fq2[...] = mix(inverse1, w1)
+    behind = mix(inverse1, parts_of(mix(a1t, parts_of(fw[:, own])))) + mix(
+        upper1, parts_of(fq1[:, own])
+    )
+    forward = dot_nn(inverse1, inverse0)
+
+    f2[:, own] = mix(forward, parts_of(collect(1))) - behind
     ag_start(f2, 2)
     ag_forward(f2, 2)
-    ag_end(f2, 2)
+    ag_end(f2, 2, 0, rows_n)
     z2 = f2[...]
-    q2 = fq2[...]
-    a2 = dot_nt(q2, z2) / total
+    q2 = parts_of(fq2[...])
+    a2 = gram_of(q2, parts_of(z2)) / total
     coef[2] = a2
-    a2t = a2.T
-    w2 = z2 - dot_nn(a2t, q2)
-    upper2, inverse2 = factor(dot_nt(w2, w2) / total)
+    w2 = z2 - mix(a2.T, q2)
+    fw[...] = w2
+    w2 = parts_of(w2)
+    upper2, inverse2 = factor(gram_of(w2, w2) / total)
     coef[3] = dot_nt(identity, upper2)
-    piece_out = dot_nn(inverse2, f2[:, own] - dot_nn(a2t, fq2[:, own]))
+    piece_out = mix(inverse2, parts_of(fw[:, own]))
     for jp in range(pb // 2):
         piece[jp] = piece_out[:, jp * 128 : (jp + 1) * 128]
     for jp in range(pb // 2):

time: 53.8 us -> 43.5 us (0.81)
  Pallas kernels: 49.6 us -> 39.2 us
    pallas_call x1, Pallas kernels: 49.6 us -> 39.2 us  [per_device(): pl.pallas_call(functools.partial(kernel, rows_n, cols_n, pb), out_shape=(...]
where the time goes in v2:
time: 43.5 us; the launch traced here: 43.2 us
  Pallas kernels  39.2 us (90%)
  local copies, waits for them, and re-layouts  2.7 us (6%)
  between operations  1.29 us (3%)
    pallas_call x1, Pallas kernels, per_device(): pl.pallas_call(functools.partial(kernel, rows_n, cols_n, pb), out_shape=(...  39.2 us
    unnamed x2, local copies, waits for them, and re-layouts  2.7 us

profile of v2, /device:TPU:1, one launch (start us, length us, event | category | flops | bytes accessed | tf_op | source)
XLA Modules:
  0.0 43.2 jit_solution(2833420744694384376)
XLA Ops:
  1.3 39.2 %shard_map.68 = (f32[4,1024]{1,0:T(4,128)}, f32[4,16,16]{2,1,0:T(8,128)}) custom-call(f32[4,1024]{1,0:T(4,128)} %start.1, f32[256,4096]{1,0:T(8,128)} %tiles.1, s32[1,256]{1,0:T(1,128)} %bitcast.2, s32[1,256]{1,0:T(1,128)} %bitcast.3, s32[1]{0:T(128)S(6)} %copy.9.counts), custom_call_target="tpu_custom_call" | custom-call | tf_op jit(solution)/shard_map/pallas_call | solution.py:365
  40.5 1.3 %copy.10 = f32[4,1024]{1,0:T(4,128)} copy(f32[4,1024]{1,0:T(4,128)} %get-tuple-element.4) | data formatting | bytes 32768
  41.8 1.4 %copy.11 = f32[4,16,16]{2,1,0:T(8,128)} copy(f32[4,16,16]{2,1,0:T(8,128)} %get-tuple-element.5) | data formatting | bytes 8192

commit v3 on v2

--- a/solution.py
+++ b/solution.py
@@ -57,9 +57,11 @@
     col = lax.broadcasted_iota(jnp.int32, (K, K), 1)
     upper = gram
     inverse = (row == col).astype(F32)
+    columns = [jnp.broadcast_to(gram[:, j : j + 1], (K, K)) for j in range(K)]
     for j in range(K):
-        ratio = upper[:, j : j + 1] / upper[j : j + 1, j : j + 1]
-        ratio = jnp.where(row > j, jnp.broadcast_to(ratio, (K, K)), 0.0)
+        ratio = jnp.where(row > j, columns[j] * (1.0 / columns[j][j : j + 1, :]), 0.0)
+        for k in range(j + 1, K):
+            columns[k] = columns[k] - ratio * columns[k][j : j + 1, :]
         upper, inverse = upper - ratio * upper[j : j + 1, :], inverse - ratio * inverse[j : j + 1, :]
     diagonal = jnp.sum(jnp.where(row == col, upper, 0.0), axis=1, keepdims=True)
     scale = 1.0 / jnp.sqrt(diagonal)
@@ -68,9 +70,9 @@
 
 def kernel(
     rows_n, cols_n, pb,
-    start, tiles, tile_rows, tile_cols, counts, basis, coef,
+    start, tiles_hbm, tile_rows, tile_cols, counts, basis, coef,
     f0, f1, f2, fq1, fw, fq2, dh, dl, lext, permt, chunk, piece, fb, sb, rs, rsib, acc,
-    ags, agf, agr, rss, rsr, sibs, sibr,
+    tiles, ags, agf, agr, rss, rsr, sibs, sibr, load,
 ):
     r = lax.axis_index("row")
     c = lax.axis_index("col")
@@ -88,6 +90,8 @@
             barrier, inc=1, device_id={"row": lax.rem(r + i, rows_n), "col": c}, device_id_type=MESH
         )
 
+    loading = pltpu.make_async_copy(tiles_hbm, tiles, load)
+    loading.start()
     lane = lax.broadcasted_iota(jnp.int32, (8, 128), 1)
 
     def lanes_of(col, row):
@@ -196,6 +200,7 @@
             dl[at, j * 128 : (j + 1) * 128] = low
         return carry
 
+    loading.wait()
     lax.fori_loop(0, pairs // 2, densify, 0)
 
     def product(ref, ph):
@@ -351,6 +356,11 @@
         rs_drain(ph)
 
 
+def store_both(basis, coef, basis_out, coef_out):
+    basis_out[...] = basis[...]
+    coef_out[...] = coef[...]
+
+
 def solution(mesh):
     rows_n = mesh.shape["row"]
     cols_n = mesh.shape["col"]
@@ -362,13 +372,13 @@
         wide = rows_n * pb * 128
         tall = cols_n * pb * BS // 2
         vmem = pl.BlockSpec(memory_space=pltpu.VMEM)
-        return pl.pallas_call(
+        results = pl.pallas_call(
             functools.partial(kernel, rows_n, cols_n, pb),
             out_shape=(
                 jax.ShapeDtypeStruct(start_block.shape, F32),
                 jax.ShapeDtypeStruct((4, K, K), F32),
             ),
-            in_specs=[vmem] * 4 + [pl.BlockSpec(memory_space=pltpu.SMEM)],
+            in_specs=[vmem, pl.BlockSpec(memory_space=pl.ANY), vmem, vmem, pl.BlockSpec(memory_space=pltpu.SMEM)],
             out_specs=(vmem, vmem),
             scratch_shapes=[pltpu.VMEM((K, length), F32)] * 6
             + [
@@ -383,6 +393,7 @@
                 pltpu.VMEM((2, rows_n, K, pb * BS), F32),
                 pltpu.VMEM((2, K, pb * BS), F32),
                 pltpu.VMEM((K, pb * BS), F32),
+                pltpu.VMEM(tiles.shape, F32),
                 pltpu.SemaphoreType.DMA((3, rows_n)),
                 pltpu.SemaphoreType.DMA((3, rows_n)),
                 pltpu.SemaphoreType.DMA((3, cols_n, rows_n)),
@@ -390,6 +401,7 @@
                 pltpu.SemaphoreType.DMA((2, rows_n)),
                 pltpu.SemaphoreType.DMA((2,)),
                 pltpu.SemaphoreType.DMA((2,)),
+                pltpu.SemaphoreType.DMA,
             ],
             compiler_params=pltpu.CompilerParams(
                 collective_id=0, has_side_effects=True, vmem_limit_bytes=56 * 2**20
@@ -401,6 +413,12 @@
             tile_cols.reshape(1, slots),
             counts,
         )
+        return pl.pallas_call(
+            store_both,
+            out_shape=tuple(jax.ShapeDtypeStruct(x.shape, F32) for x in results),
+            in_specs=[vmem, vmem],
+            out_specs=(vmem, vmem),
+        )(*results)
 
     return jax.shard_map(
         per_device,

time: 43.5 us -> 38.9 us (0.89)
  local copies, waits for them, and re-layouts: 2.7 us -> 0 us
  Pallas kernels: 39.2 us -> 37.3 us
    pallas_call x1, Pallas kernels: 39.2 us -> 35.9 us  [per_device(): pl.pallas_call(functools.partial(kernel, rows_n, cols_n, pb), out_shape=(...]
    unnamed x2 -> x0, local copies, waits for them, and re-layouts: 2.7 us -> none
    pallas_call x0 -> x1, Pallas kernels: none -> 1.4 us  [per_device(): pl.pallas_call(store_both, out_shape=tuple((jax.ShapeDtypeStruct(x.shape,...]
where the time goes in v3:
time: 38.9 us; the launch traced here: 38.6 us
  Pallas kernels  37.3 us (96%)
  between operations  1.29 us (3%)
    pallas_call x1, Pallas kernels, per_device(): pl.pallas_call(functools.partial(kernel, rows_n, cols_n, pb), out_shape=(...  35.9 us
    pallas_call x1, Pallas kernels, per_device(): pl.pallas_call(store_both, out_shape=tuple((jax.ShapeDtypeStruct(x.shape,...  1.4 us

profile of v3, /device:TPU:1, one launch (start us, length us, event | category | flops | bytes accessed | tf_op | source)
XLA Modules:
  0.0 38.6 jit_solution(8427238942661292071)
XLA Ops:
  1.3 35.9 %shard_map.68 = (f32[4,1024]{1,0:T(4,128)}, f32[4,16,16]{2,1,0:T(8,128)}) custom-call(f32[4,1024]{1,0:T(4,128)} %start.1, f32[256,4096]{1,0:T(8,128)} %tiles_hbm.1, s32[1,256]{1,0:T(1,128)} %bitcast.2, s32[1,256]{1,0:T(1,128)} %bitcast.3, s32[1]{0:T(128)S(6)} %copy.7.counts), custom_call_target="tpu_custom_call" | custom-call | tf_op jit(solution)/shard_map/pallas_call | solution.py:375
  37.2 1.4 %shard_map.69 = (f32[4,1024]{1,0:T(4,128)}, f32[4,16,16]{2,1,0:T(8,128)}) custom-call(f32[4,1024]{1,0:T(4,128)} %get-tuple-element.4.basis, f32[4,16,16]{2,1,0:T(8,128)} %get-tuple-element.5.coef), custom_call_target="tpu_custom_call" | custom-call | tf_op jit(solution)/shard_map/pallas_call | solution.py:416

commit v4 on v3

--- a/solution.py
+++ b/solution.py
@@ -203,7 +203,11 @@
     loading.wait()
     lax.fori_loop(0, pairs // 2, densify, 0)
 
-    def product(ref, ph):
+    wide = lax.broadcasted_iota(jnp.int32, (K, 128), 1)
+    low_half = wide < 64
+    group = 4 if rows_n % 4 == 0 else 1
+
+    def back_product(ref, ph):
         across = jnp.concatenate([ref[:, lanes_of(i, r)] for i in range(cols_n)], axis=1)
         parts = jnp.concatenate(split3(across), axis=0)
         even = dot_nt(parts, permt[0]).astype(BF16)
@@ -211,28 +215,11 @@
         lrow = jnp.concatenate(
             [x[i * K : (i + 1) * K] for i in range(3) for x in (even, odd)], axis=0
         )
-        wide = lax.broadcasted_iota(jnp.int32, (K, 128), 1)
-        low_half = wide < 64
-
-        group = 4 if rows_n % 4 == 0 else 1
-
         def back(step, carry):
             first = rows_n - (step + 1) * group
             for g in range(group - 1, -1, -1):
                 target = first + g
                 at = pl.ds(pl.multiple_of(target * pb * 128, 128), pb * 128)
-                v = ref[:, lanes_of(c, target)]
-                extended = []
-                for jp in range(pb // 2):
-                    x = v[:, jp * 128 : (jp + 1) * 128]
-                    y = pltpu.roll(x, 64, 1)
-                    extended.append(
-                        jnp.concatenate([jnp.where(low_half, x, 0.0), jnp.where(low_half, 0.0, y)], axis=0)
-                    )
-                    extended.append(
-                        jnp.concatenate([jnp.where(low_half, y, 0.0), jnp.where(low_half, 0.0, x)], axis=0)
-                    )
-                lext[:, at] = jnp.concatenate(split3(jnp.concatenate(extended, axis=1)), axis=0)
                 x = dot_nn(lrow, dh[:, at])
                 y = dot_nn(lrow[: 4 * K], dl[:, at])
                 z = x[4 * K :] + (x[2 * K : 4 * K] + y[2 * K :]) + y[: 2 * K] + x[: 2 * K]
@@ -256,6 +243,27 @@
 
         lax.fori_loop(0, rows_n // group, back, 0)
 
+    def front_product(ref, ph):
+        def extend(step, carry):
+            for g in range(group):
+                target = step * group + g
+                at = pl.ds(pl.multiple_of(target * pb * 128, 128), pb * 128)
+                v = ref[:, lanes_of(c, target)]
+                extended = []
+                for jp in range(pb // 2):
+                    x = v[:, jp * 128 : (jp + 1) * 128]
+                    y = pltpu.roll(x, 64, 1)
+                    extended.append(
+                        jnp.concatenate([jnp.where(low_half, x, 0.0), jnp.where(low_half, 0.0, y)], axis=0)
+                    )
+                    extended.append(
+                        jnp.concatenate([jnp.where(low_half, y, 0.0), jnp.where(low_half, 0.0, x)], axis=0)
+                    )
+                lext[:, at] = jnp.concatenate(split3(jnp.concatenate(extended, axis=1)), axis=0)
+            return carry
+
+        lax.fori_loop(0, rows_n // group, extend, 0)
+
         x = dot_nt(dh[...], lext[...]).T
         y = dot_nt(dl[...], lext[: 4 * K, :]).T
         z = x[4 * K :] + (x[2 * K : 4 * K] + y[2 * K :]) + y[: 2 * K] + x[: 2 * K]
@@ -296,9 +304,10 @@
         lax.broadcasted_iota(jnp.int32, (K, K), 0) == lax.broadcasted_iota(jnp.int32, (K, K), 1)
     ).astype(F32)
 
+    ag_end(f0, 0, 0, 1)
+    back_product(f0, 0)
     ag_forward(f0, 0)
-    ag_end(f0, 0, 0, 1)
-    product(f0, 0)
+    front_product(f0, 0)
     ag_end(f0, 0, 1, rows_n)
     v = parts_of(f0[...])
     unused, inverse0 = factor(gram_of(v, v) / total)
@@ -306,9 +315,10 @@
 
     f1[:, own] = collect(0)
     ag_start(f1, 1)
+    ag_end(f1, 1, 0, 1)
+    back_product(f1, 1)
     ag_forward(f1, 1)
-    ag_end(f1, 1, 0, 1)
-    product(f1, 1)
+    front_product(f1, 1)
     ag_end(f1, 1, 1, rows_n)
     z1 = mix(inverse0, parts_of(f1[...]))
     fw[...] = z1

time: 38.9 us -> 38 us (0.977)
  Pallas kernels: 37.3 us -> 36.4 us
    pallas_call x1, Pallas kernels: 35.9 us -> 35 us  [per_device(): pl.pallas_call(functools.partial(kernel, rows_n, cols_n, pb), out_shape=(...]
where the time goes in v4:
time: 38 us; the launch traced here: 37.7 us
  Pallas kernels  36.4 us (96%)
  between operations  1.29 us (3%)
    pallas_call x1, Pallas kernels, per_device(): pl.pallas_call(functools.partial(kernel, rows_n, cols_n, pb), out_shape=(...  35 us
    pallas_call x1, Pallas kernels, per_device(): pl.pallas_call(store_both, out_shape=tuple((jax.ShapeDtypeStruct(x.shape,...  1.4 us

profile of v4, /device:TPU:1, one launch (start us, length us, event | category | flops | bytes accessed | tf_op | source)
XLA Modules:
  0.0 37.7 jit_solution(11001827236991225414)
XLA Ops:
  1.3 35.0 %shard_map.68 = (f32[4,1024]{1,0:T(4,128)}, f32[4,16,16]{2,1,0:T(8,128)}) custom-call(f32[4,1024]{1,0:T(4,128)} %start.1, f32[256,4096]{1,0:T(8,128)} %tiles_hbm.1, s32[1,256]{1,0:T(1,128)} %bitcast.2, s32[1,256]{1,0:T(1,128)} %bitcast.3, s32[1]{0:T(128)S(6)} %copy.7.counts), custom_call_target="tpu_custom_call" | custom-call | tf_op jit(solution)/shard_map/pallas_call | solution.py:385
  36.3 1.4 %shard_map.69 = (f32[4,1024]{1,0:T(4,128)}, f32[4,16,16]{2,1,0:T(8,128)}) custom-call(f32[4,1024]{1,0:T(4,128)} %get-tuple-element.4.basis, f32[4,16,16]{2,1,0:T(8,128)} %get-tuple-element.5.coef), custom_call_target="tpu_custom_call" | custom-call | tf_op jit(solution)/shard_map/pallas_call | solution.py:426
